TPU v7x, 256 devices: a whole 4x4x8 slice. The times are simulated.
256 devices in a mesh: blk: 32 (over z, y_hi, core), slab: 8 (over x, y_lo).
Axes of the slice: x: 4, y: 4 (y_hi: 2, y_lo: 2; y = y_hi * 2 + y_lo), z: 8, core: 2. Of those that a mesh axis runs over, the one named last changes fastest.
Arguments:
- queries: bfloat16 [512, 768], P('blk'), may hold values from -64 to 64
- teacher_weight: bfloat16 [512, 200], P('blk'), may hold values from 0.0009994507 to 1
- cand_ids: int32 [512, 200], P('blk'), may hold values from 0 to 262143, as said below
- passages: bfloat16 [262144, 768], P(('blk', 'slab')), may hold values from -8 to 8
Outputs:
- loss: float32 [512], P('blk')
- grad_query: float32 [512, 768], P(('blk', 'slab'))
Inputs may be any that keep to these rules, and one draw needn't show every extreme that they name: `cand_ids`: each row holds 200 distinct ids; the k-th lies in the k-th of 200 consecutive ranges of 1310 ids (the last range runs to the end).
All inputs are finite; a program needn't handle non-finite values.
Results may differ from a plain program's by a relative error of at most 0.012.
Values may be sent and summed in bfloat16 or wider, within the bound.
A program may use at most 64 MiB of HBM per device.

v0:
```python
import math

import jax
import jax.numpy as jnp
from jax import lax
from jax.sharding import PartitionSpec as P


def shards(queries, teacher_weight, cand_ids, passages):
    logit_scale = 3.0 / math.sqrt(passages.shape[1])
    tile_rows = queries.shape[0]
    width = passages.shape[0]
    num_cand = cand_ids.shape[1]
    all_queries, all_weights = (
        lax.all_gather(queries, "blk", axis=0, tiled=True),
        lax.all_gather(teacher_weight, "blk", axis=0, tiled=True),
    )
    all_ids = lax.all_gather(cand_ids, "blk", axis=0, tiled=True)
    rows = all_queries.shape[0]
    stride = width * lax.axis_size("blk") * lax.axis_size("slab") // num_cand
    window = min(num_cand, (width - 1) // stride + 2)
    offset = (lax.axis_index("blk") * lax.axis_size("slab") + lax.axis_index("slab")) * width
    first_range = jnp.minimum(offset // stride, num_cand - window)
    scores = logit_scale * lax.dot_general(
        all_queries, passages, (((1,), (1,)), ((), ())), preferred_element_type=jnp.float32
    )
    weights = all_weights.astype(jnp.float32)
    tprob = weights / jnp.sum(weights, axis=1, keepdims=True)
    win_ids = lax.dynamic_slice_in_dim(all_ids, first_range, window, 1)
    win_prob = lax.dynamic_slice_in_dim(tprob, first_range, window, 1)
    local_ids = win_ids - offset
    inside = (local_ids >= 0) & (local_ids < width)
    safe_ids = jnp.where(inside, local_ids, 0)
    picked = jnp.take_along_axis(scores, safe_ids, axis=1)
    teacher_part = jnp.sum(jnp.where(inside, win_prob * picked, jnp.float32(0.0)), axis=1)
    local_peak = jnp.max(scores, axis=1)
    peak = lax.pmax(local_peak, ("blk", "slab"))
    partial_total = jnp.sum(jnp.exp(scores - peak[:, None]), axis=1)
    total, teacher_sum = lax.psum((partial_total, teacher_part), ("blk", "slab"))
    lse = peak + jnp.log(total)
    loss_all = jnp.sum(tprob * jnp.log(tprob), axis=1) - teacher_sum + lse
    loss = lax.dynamic_slice_in_dim(loss_all, lax.axis_index("blk") * tile_rows, tile_rows, 0)
    columns = lax.broadcasted_iota(jnp.int32, (rows, width), 1)
    target = jnp.zeros((rows, width), jnp.float32)
    for column in range(window):
        target = target + jnp.where(
            columns == local_ids[:, column : column + 1],
            win_prob[:, column : column + 1],
            jnp.float32(0.0),
        )
    delta = (jnp.exp(scores - lse[:, None]) - target).astype(jnp.bfloat16)
    grad_query = lax.psum_scatter(
        logit_scale * jnp.dot(delta, passages, preferred_element_type=jnp.float32),
        ("blk", "slab"),
        scatter_dimension=0,
        tiled=True,
    )
    return (loss, grad_query)


def solution(mesh):
    return jax.shard_map(
        shards,
        mesh=mesh,
        in_specs=(P("blk", None), P("blk", None), P("blk", None), P(("blk", "slab"), None)),
        out_specs=(P("blk"), P(("blk", "slab"), None)),
        check_vma=False,
    )
```

profile of v0, /device:TPU:8, one launch (start us, length us, event | category | flops | bytes accessed | tf_op | source)
XLA Modules:
  0.0 572.7 jit_solution(17340167876856641125)
XLA Ops:
  7.2 0.0 copy-start
  7.2 0.0 all-reduce.4.cloned.1.call-start
  7.3 45.0 %all_gather.9 = bf16[512,200]{1,0:T(8,128)(2,1)S(1)} all-gather(bf16[16,200]{1,0:T(8,128)(2,1)} %param.5), channel_id=1, replica_groups=mesh['blk'=32,'slab'=8] {'blk'}, dimensions={0}, use_global_device_ids=true | all-gather | bytes 211200 | tf_op jit(solution)/shard_map/all_gather | solution.py:16
  52.3 0.1 convert_reduce_fusion
  52.4 0.3 fusion.6
  52.7 39.1 %all_gather.11 = bf16[512,768]{1,0:T(8,128)(2,1)S(1)} all-gather(bf16[16,768]{1,0:T(8,128)(2,1)} %param.4), channel_id=1, replica_groups=mesh['blk'=32,'slab'=8] {'blk'}, dimensions={0}, use_global_device_ids=true | all-gather | bytes 811008 | tf_op jit(solution)/shard_map/all_gather | solution.py:15
  91.8 2.4 fusion.8
  94.2 75.4 %pmax.7 = f32[512]{0:T(512)S(1)} all-reduce(f32[512]{0:T(512)S(1)} %get-tuple-element.14), channel_id=1, replica_groups=mesh['blk'=32,'slab'=8] {'blk','slab'}, use_global_device_ids=true, to_apply=%region_5.6 | all-reduce | flops 512 | bytes 4096 | tf_op jit(solution)/shard_map/pmax | solution.py:37
  169.6 0.0 copy-done.1
  169.6 41.5 %all_gather.10 = s32[512,200]{1,0:T(8,128)S(1)} all-gather(s32[16,200]{1,0:T(8,128)S(1)} %copy-done.1), channel_id=1, replica_groups=mesh['blk'=32,'slab'=8] {'blk'}, dimensions={0}, use_global_device_ids=true | all-gather | bytes 422400 | tf_op jit(solution)/shard_map/all_gather | solution.py:18
  211.1 0.2 bitcast_or_fusion
  211.3 0.2 reshape.17
  211.5 2.0 exponential_reduce_fusion
  213.5 17.5 %gather_fusion = f32[1024]{0:T(1024)S(1)} fusion(f32[512,1024]{1,0:T(8,128)} %get-tuple-element.15, s32[1024]{0:T(1024)S(1)} %reshape.17), kind=kCustom, calls=%fused_computation | custom fusion | bytes 16384 | tf_op jit(solution)/shard_map/jit(take_along_axis)/gather | solution.py:34
  231.0 0.2 reshape.20
  231.2 0.3 slice_reduce_fusion.1
  231.5 0.3 select_reduce_fusion
  231.8 0.4 dynamic-slice_reduce_fusion.1
  232.2 72.3 %all-reduce.1 = (f32[512]{0:T(512)S(1)}, f32[512]{0:T(512)S(1)}) all-reduce(f32[512]{0:T(512)S(1)} %exponential_reduce_fusion, f32[512]{0:T(512)S(1)} %select_reduce_fusion), channel_id=1, replica_groups=mesh['blk'=32,'slab'=8] {'blk','slab'}, use_global_device_ids=true, to_apply=%region_7.8 | all-reduce | flops 1024 | bytes 8192 | tf_op jit(solution)/shard_map/psum | solution.py:39
  304.5 4.3 convolution_multiply_fusion.1
  308.8 0.0 all-reduce.4.cloned.1.call-update
  308.8 0.6 dynamic_slice.11
  309.4 255.1 %all-reduce.4.cloned.1.call-done = f32[512,768]{1,0:T(8,128)} async-done(((f32[512,768]{1,0:T(8,128)}), f32[512,768]{1,0:T(8,128)}) %all-reduce.4.cloned.1.call-update) | async-done | bytes 1572880
  564.5 1.3 constant_dynamic-slice_fusion
  (3 shorter events, 0.0 us)
Async XLA Ops:
  7.2 84.7 %copy-start = (bf16[1024,768]{1,0:T(8,128)(2,1)S(1)}, bf16[1024,768]{1,0:T(8,128)(2,1)}, u32[]{:S(2)}) copy-start(bf16[1024,768]{1,0:T(8,128)(2,1)} %param.7) | copy-start | bytes 4718596
  7.2 557.3 %all-reduce.4.cloned.1.call-start = ((), (), s32[]{:S(2)}) async-start(), calls=%async_computation | async-start | bytes 3145728
  91.8 77.8 %copy-start.1 = (s32[16,200]{1,0:T(8,128)S(1)}, s32[16,200]{1,0:T(8,128)}, u32[]{:S(2)}) copy-start(s32[16,200]{1,0:T(8,128)} %param.6) | copy-start | bytes 38404
Sparse Core Ops, SparseCore 0:
  308.9 255.5 all-reduce.3
where the time goes:
time: 574 us; the launch traced here: 573 us
  blocking collectives  273 us (48%)
  waiting for transfers between devices  255 us (44%)
  local copies, waits for them, and re-layouts  20.5 us (4%)
  between operations  14.1 us (2%)
  matrix products  6.65 us (1%)
    unnamed x2, waiting for transfers between devices  255 us
    pmax x1, blocking collectives, shards(): peak = lax.pmax(local_peak, ('blk', 'slab'))  75.4 us
    psum x1, blocking collectives, shards(): lax.psum((partial_total, teacher_part), ('blk', 'slab'))  72.3 us
    all_gather x1, blocking collectives, shards(): lax.all_gather(teacher_weight, 'blk', axis=0, tiled=True)  45 us
    all_gather x1, blocking collectives, shards(): all_ids = lax.all_gather(cand_ids, 'blk', axis=0, tiled=True)  41.5 us
    all_gather x1, blocking collectives, shards(): lax.all_gather(queries, 'blk', axis=0, tiled=True)  39.1 us
    gather x3, local copies, waits for them, and re-layouts, shards(): picked = jnp.take_along_axis(scores, safe_ids, axis=1)  17.9 us
  transfers between devices with their start and end apart: 1, of which 1 were waited for; matrix products, arithmetic and copies ran while one was open for 0% of the time, Pallas kernels for 0%

commit v1 on v0

v1 whole, which is shorter than its diff:
```python
import functools
import math

import jax
import jax.numpy as jnp
from jax import lax
from jax.experimental import pallas as pl
from jax.experimental.pallas import tpu as pltpu
from jax.sharding import PartitionSpec as P

MESH = pl.DeviceIdType.MESH
F32 = jnp.float32
BF16 = jnp.bfloat16
I32 = jnp.int32
FAR_FIRST = (4, 3, 5, 2, 6, 1, 7, 0)


def position():
    blk = lax.axis_index("blk")
    slab = lax.axis_index("slab")
    z = blk // 4
    y = ((blk // 2) % 2) * 2 + slab % 2
    return slab // 2, y, z, blk % 2


def device(x, y, z, core):
    return {"blk": (z * 2 + y // 2) * 2 + core, "slab": x * 2 + y % 2}


def iota(shape, dim):
    return lax.broadcasted_iota(I32, shape, dim)


def split3(value):
    first = value.astype(BF16)
    rest = value - first.astype(F32)
    second = rest.astype(BF16)
    third = (rest - second.astype(F32)).astype(BF16)
    return first, second, third


def kernel(
    stride,
    scale,
    q_ref,
    w_ref,
    id_ref,
    pas_ref,
    loss_ref,
    grad_ref,
    pas,
    queries,
    cands,
    cand_out,
    perm_ref,
    prob_out,
    exp_out,
    stat_out,
    prob_in,
    exp_in,
    stat_in,
    z_out,
    z_in,
    zstat_out,
    zstat_in,
    pas_sem,
    q_sems,
    c_sems,
    prob_sems,
    exp_sems,
    stat_sems,
    z_sems,
    zstat_sems,
):
    x, y, z, core = position()
    y_hi, y_lo = y // 2, y % 2
    slab = x * 2 + y_lo
    width = pas_ref.shape[0]
    num_cand = id_ref.shape[1]
    plane = width * 32
    per_plane = plane // stride

    gather_to = [
        (device(x, y if dy == 0 else 3 - y, (z + d) % 8, core), dy * 8 + (8 - d) % 8, d)
        for d in FAR_FIRST
        for dy in (0, 1)
        if (d, dy) != (0, 0)
    ]
    plane_to = [
        (
            device((x + ex) % 4, (y + ey) % 4, z, core),
            ex * 4 + ey,
            ((4 - ex) % 4) * 4 + (4 - ey) % 4,
            (((y + ey) % 4) // 2 + y_hi) % 2,
        )
        for ex in (2, 1, 3, 0)
        for ey in (2, 1, 3, 0)
        if (ex, ey) != (0, 0)
    ]
    z_to = [(device(x, y, (z + d) % 8, core), d, (8 - d) % 8) for d in FAR_FIRST if d]
    other = device(x, y, z, 1 - core)

    barrier = pltpu.get_barrier_semaphore()
    greeted = [other] + [p[0] for p in plane_to]
    greeted += [p[0] for p in gather_to if p[2] != 0]
    for target in greeted:
        pl.semaphore_signal(barrier, inc=1, device_id=target, device_id_type=MESH)

    load = pltpu.make_async_copy(pas_ref, pas.at[0], pas_sem.at[0])
    load.start()

    weights = w_ref[...].astype(F32)
    weight_sum = jnp.sum(weights, axis=1, keepdims=True)
    own_prob = weights / weight_sum
    entropy = jnp.sum(own_prob * jnp.log(own_prob), axis=1, keepdims=True)
    pad = 256 - num_cand
    wide_w = jnp.concatenate([weights, jnp.zeros((16, pad), F32)], axis=1)
    wide_id = jnp.concatenate([id_ref[...], jnp.zeros((16, pad), I32)], axis=1)
    s1, s2, s3 = split3(weight_sum)
    lane32 = iota((16, 32), 1)
    sums = jnp.where(
        lane32 == 0,
        s1.astype(F32),
        jnp.where(lane32 == 1, s2.astype(F32), jnp.where(lane32 == 2, s3.astype(F32), 0.0)),
    )
    for zz in range(8):
        lo = per_plane * zz
        ids = jnp.maximum(wide_id[:, lo : lo + 32] - lo * stride, 0)
        high = (ids >> 8).astype(F32)
        low = (ids & 255).astype(F32)
        cand_out[zz] = jnp.concatenate([high, low, wide_w[:, lo : lo + 32], sums], axis=1).astype(BF16)
    cands[0] = cand_out[z]
    queries[0] = q_ref[...]

    p_row = iota((256, 1), 0)
    p_x = (x + (p_row >> 6)) & 3
    p_y = (y + ((p_row >> 4) & 3)) & 3
    p_dy = ((p_y >> 1) + y_hi) & 1
    p_n = p_dy * 128 + ((p_row >> 1) & 7) * 16 + (p_x * 2 + (p_y & 1)) * 2 + (p_row & 1)
    hot = (iota((256, 256), 1) == p_n).astype(F32)
    perm_ref[...] = hot.astype(BF16)

    pl.semaphore_wait(barrier, len(greeted))

    swap = pltpu.make_async_remote_copy(
        pas_ref, pas.at[1], pas_sem.at[1], pas_sem.at[2], device_id=other, device_id_type=MESH
    )
    swap.start()
    sent = []
    cand_copies, q_copies = {}, {}
    for i, (target, slot, d) in enumerate(gather_to):
        copy = pltpu.make_async_remote_copy(
            cand_out.at[(z + d) % 8],
            cands.at[slot],
            c_sems.at[0, i],
            c_sems.at[1, i],
            device_id=target,
            device_id_type=MESH,
        )
        copy.start()
        cand_copies[i] = copy
    for i, (target, slot, d) in enumerate(gather_to):
        copy = pltpu.make_async_remote_copy(
            q_ref,
            queries.at[slot],
            q_sems.at[0, i],
            q_sems.at[1, i],
            device_id=target,
            device_id_type=MESH,
        )
        copy.start()
        q_copies[i] = copy
    sent += list(cand_copies.values()) + list(q_copies.values())

    offsets = [((((z * 2 + y_hi) * 2 + c) * 8) + slab) * width for c in (core, 1 - core)]
    firsts = [jnp.minimum(off // stride, num_cand - 2) - per_plane * z for off in offsets]
    out_lane = iota((1, 128), 1)
    target_lane = jnp.where((out_lane >= 12) & (out_lane < 15), 96 + out_lane - 12, -1)
    for rho in range(2):
        for c in range(2):
            for field in range(3):
                target_lane = jnp.where(
                    out_lane == (rho * 2 + c) * 3 + field, field * 32 + firsts[rho] + c, target_lane
                )
    pick = (iota((128, 128), 0) == target_lane).astype(F32).astype(BF16)
    for copy in cand_copies.values():
        copy.wait_recv()
    picked = jnp.dot(cands[...].reshape(256, 128), pick, preferred_element_type=F32).astype(BF16)
    picked = jnp.dot(perm_ref[...], picked, preferred_element_type=F32)
    total_w = picked[:, 12:13] + picked[:, 13:14] + picked[:, 14:15]
    load.wait()
    column = iota((256, width), 1).astype(F32)
    prob_sum = None
    swap.wait_recv()
    for rho in range(2):
        shift = (per_plane * stride * z - offsets[rho]).astype(F32)
        dense = None
        for c in range(2):
            at = (rho * 2 + c) * 3
            local = picked[:, at : at + 1] * 256.0 + picked[:, at + 1 : at + 2] + shift
            prob = picked[:, at + 2 : at + 3] / total_w
            term = jnp.where(column == local, prob, 0.0)
            dense = term if dense is None else dense + term
        part = jnp.dot(dense.astype(BF16), pas[rho], preferred_element_type=F32)
        prob_sum = part if prob_sum is None else prob_sum + part
    prob_out[...] = prob_sum.astype(BF16).reshape(16, 16, -1)
    prob_copies = []
    for i, (target, group, slot, _) in enumerate(plane_to):
        copy = pltpu.make_async_remote_copy(
            prob_out.at[group],
            prob_in.at[slot],
            prob_sems.at[0, i],
            prob_sems.at[1, i],
            device_id=target,
            device_id_type=MESH,
        )
        copy.start()
        prob_copies.append(copy)
    sent += prob_copies

    for copy in q_copies.values():
        copy.wait_recv()
    depth = q_ref.shape[1]
    rows = jnp.dot(perm_ref[...], queries[...].reshape(256, depth), preferred_element_type=F32)
    rows16 = rows.astype(BF16)
    teacher = scale * jnp.sum(rows * prob_sum, axis=1, keepdims=True)
    nt = (((1,), (1,)), ((), ()))
    scores = [
        scale * lax.dot_general(rows16, pas[rho], nt, preferred_element_type=F32) for rho in range(2)
    ]
    peak = jnp.maximum(
        jnp.max(scores[0], axis=1, keepdims=True), jnp.max(scores[1], axis=1, keepdims=True)
    )
    exps = [jnp.exp(s - peak) for s in scores]
    total = jnp.sum(exps[0], axis=1, keepdims=True) + jnp.sum(exps[1], axis=1, keepdims=True)
    mixed = jnp.dot(exps[0].astype(BF16), pas[0], preferred_element_type=F32) + jnp.dot(
        exps[1].astype(BF16), pas[1], preferred_element_type=F32
    )
    exp_out[...] = mixed.astype(BF16).reshape(16, 16, depth)
    mask = perm_ref[...].astype(F32) > 0.5
    for k, stat in enumerate((peak, total, teacher)):
        lanes = jnp.sum(jnp.where(mask, stat, 0.0), axis=0, keepdims=True)
        stat_out[0, k : k + 1, :] = lanes[:, :128]
        stat_out[1, k : k + 1, :] = lanes[:, 128:]
    exp_copies, stat_copies = [], []
    for i, (target, group, slot, dy) in enumerate(plane_to):
        copy = pltpu.make_async_remote_copy(
            stat_out.at[dy],
            stat_in.at[slot],
            stat_sems.at[0, i],
            stat_sems.at[1, i],
            device_id=target,
            device_id_type=MESH,
        )
        copy.start()
        stat_copies.append(copy)
        copy = pltpu.make_async_remote_copy(
            exp_out.at[group],
            exp_in.at[slot],
            exp_sems.at[0, i],
            exp_sems.at[1, i],
            device_id=target,
            device_id_type=MESH,
        )
        copy.start()
        exp_copies.append(copy)
    sent += exp_copies + stat_copies

    stat_in[0] = stat_out[0]
    for copy in prob_copies:
        copy.wait_recv()
    prob_rows = prob_out[0].astype(F32)
    for i in range(1, 16):
        prob_rows = prob_rows + prob_in[i].astype(F32)
    for copy in stat_copies:
        copy.wait_recv()
    peaks = jnp.concatenate([stat_in[i, 0:1, :] for i in range(16)], axis=0)
    totals = jnp.concatenate([stat_in[i, 1:2, :] for i in range(16)], axis=0)
    teachers = jnp.concatenate([stat_in[i, 2:3, :] for i in range(16)], axis=0)
    peak = jnp.max(peaks, axis=0, keepdims=True)
    share = jnp.exp(peaks - peak)
    total = jnp.sum(totals * share, axis=0, keepdims=True)
    teacher = jnp.sum(teachers, axis=0, keepdims=True)
    zstat_out[0:1, :] = peak
    zstat_out[1:2, :] = total
    zstat_out[2:3, :] = teacher
    zstat_copies = []
    for i, (target, d, slot) in enumerate(z_to):
        copy = pltpu.make_async_remote_copy(
            zstat_out,
            zstat_in.at[slot],
            zstat_sems.at[0, i],
            zstat_sems.at[1, i],
            device_id=target,
            device_id_type=MESH,
        )
        copy.start()
        zstat_copies.append(copy)
    row = iota((16, 128), 0)
    own_lane = iota((16, 128), 1) == (row >> 1) * 16 + slab * 2 + (row & 1)
    columns = [
        jnp.sum(jnp.where(own_lane, share[i : i + 1, :], 0.0), axis=1, keepdims=True) for i in range(16)
    ]
    for copy in exp_copies:
        copy.wait_recv()
    exp_rows = exp_out[0].astype(F32) * columns[0]
    for i in range(1, 16):
        exp_rows = exp_rows + exp_in[i].astype(F32) * columns[i]

    stacked = jnp.concatenate(
        [part[:, b * 128 : (b + 1) * 128] for part in (exp_rows, prob_rows) for b in range(6)], axis=0
    ).astype(BF16)
    o = iota((256, 1), 0)
    j = o & 31
    part = (j >= 12).astype(I32)
    jj = j - 12 * part
    source = part * 96 + (jj >> 1) * 16 + (o >> 5) * 2 + (jj & 1)
    source = jnp.where(j < 24, source, -1)
    order = (iota((256, 192), 1) == source).astype(F32).astype(BF16)
    z_out[...] = jnp.dot(order, stacked, preferred_element_type=F32).astype(BF16).reshape(8, 32, 128)
    z_copies = []
    for i, (target, d, slot) in enumerate(z_to):
        copy = pltpu.make_async_remote_copy(
            z_out.at[d],
            z_in.at[slot],
            z_sems.at[0, i],
            z_sems.at[1, i],
            device_id=target,
            device_id_type=MESH,
        )
        copy.start()
        z_copies.append(copy)
    sent += zstat_copies + z_copies

    zstat_in[0] = zstat_out[...]
    entropy_lanes = jnp.sum(
        jnp.where(iota((16, 16), 0) == iota((16, 16), 1), entropy, 0.0), axis=0, keepdims=True
    )
    for copy in zstat_copies:
        copy.wait_recv()

    def gathered(k):
        return jnp.concatenate(
            [zstat_in[s, k : k + 1, ((8 - s) % 8) * 16 : ((8 - s) % 8) * 16 + 16] for s in range(8)], axis=0
        )

    peaks, totals, teachers = gathered(0), gathered(1), gathered(2)
    peak = jnp.max(peaks, axis=0, keepdims=True)
    total = jnp.sum(totals * jnp.exp(peaks - peak), axis=0, keepdims=True)
    lse = peak + jnp.log(total)
    loss_ref[...] = entropy_lanes - jnp.sum(teachers, axis=0, keepdims=True) + lse
    share = jnp.exp(peaks - lse)
    row = iota((16, 16), 0)
    own_lane = iota((16, 16), 1) == slab * 2 + (row & 1)
    columns = [
        jnp.sum(jnp.where(own_lane, share[s : s + 1, :], 0.0), axis=1, keepdims=True) for s in range(8)
    ]
    for copy in z_copies:
        copy.wait_recv()
    z_in[0] = z_out[0]
    result = None
    for s in range(8):
        block = z_in[s].astype(F32)
        term = block[0:12] * columns[s][0:12] - block[12:24]
        result = term if result is None else result + term
    result = scale * result
    for b in range(6):
        grad_ref[:, b * 128 : (b + 1) * 128] = result[2 * b : 2 * b + 2]

    swap.wait_send()
    for copy in sent:
        copy.wait_send()


def shards(queries, teacher_weight, cand_ids, passages):
    rows, depth = queries.shape
    width = passages.shape[0]
    num_cand = cand_ids.shape[1]
    stride = width * 256 // num_cand
    scale = 3.0 / math.sqrt(depth)
    vmem = pl.BlockSpec(memory_space=pltpu.VMEM)
    dma = pltpu.SemaphoreType.DMA
    loss, grad = pl.pallas_call(
        functools.partial(kernel, stride, scale),
        out_shape=(jax.ShapeDtypeStruct((1, rows), F32), jax.ShapeDtypeStruct((2, depth), F32)),
        in_specs=[vmem, vmem, vmem, pl.BlockSpec(memory_space=pl.ANY)],
        out_specs=(vmem, vmem),
        scratch_shapes=[
            pltpu.VMEM((2, width, depth), BF16),
            pltpu.VMEM((16, 16, depth), BF16),
            pltpu.VMEM((16, 16, 128), BF16),
            pltpu.VMEM((8, 16, 128), BF16),
            pltpu.VMEM((256, 256), BF16),
            pltpu.VMEM((16, 16, depth), BF16),
            pltpu.VMEM((16, 16, depth), BF16),
            pltpu.VMEM((2, 8, 128), F32),
            pltpu.VMEM((16, 16, depth), BF16),
            pltpu.VMEM((16, 16, depth), BF16),
            pltpu.VMEM((16, 8, 128), F32),
            pltpu.VMEM((8, 32, 128), BF16),
            pltpu.VMEM((8, 32, 128), BF16),
            pltpu.VMEM((8, 128), F32),
            pltpu.VMEM((8, 8, 128), F32),
            dma((3,)),
            dma((2, 15)),
            dma((2, 15)),
            dma((2, 15)),
            dma((2, 15)),
            dma((2, 15)),
            dma((2, 7)),
            dma((2, 7)),
        ],
        compiler_params=pltpu.CompilerParams(
            collective_id=0, has_side_effects=True, vmem_limit_bytes=48 * 1024 * 1024
        ),
    )(queries, teacher_weight, cand_ids, passages)
    return (loss.reshape(rows), grad)


def solution(mesh):
    return jax.shard_map(
        shards,
        mesh=mesh,
        in_specs=(P("blk", None), P("blk", None), P("blk", None), P(("blk", "slab"), None)),
        out_specs=(P("blk"), P(("blk", "slab"), None)),
        check_vma=False,
    )
```

time: 574 us -> 45.2 us (0.08)
  blocking collectives: 273 us -> 0 us
  waiting for transfers between devices: 255 us -> 0 us
  Pallas kernels: 0 us -> 39.2 us
  local copies, waits for them, and re-layouts: 20.5 us -> 4.66 us
  between operations: 14.1 us -> 0.65 us
  matrix products: 6.65 us -> 0 us
    unnamed x2 -> x0, waiting for transfers between devices: 255 us -> none
    all_gather x3 -> x0, blocking collectives: 126 us -> none  [the longest x1 45 us: shards(): lax.all_gather(teacher_weight, 'blk', axis=0, tiled=True)]
    pmax x1 -> x0, blocking collectives: 75.4 us -> none  [shards(): peak = lax.pmax(local_peak, ('blk', 'slab'))]
    psum x1 -> x0, blocking collectives: 72.3 us -> none  [shards(): lax.psum((partial_total, teacher_part), ('blk', 'slab'))]
    pallas_call x0 -> x1, Pallas kernels: none -> 39.2 us  [shards(): pl.pallas_call(functools.partial(kernel, stride, scale), out_shape=(jax.S...]
    gather x3 -> x0, local copies, waits for them, and re-layouts: 17.9 us -> none  [shards(): picked = jnp.take_along_axis(scores, safe_ids, axis=1)]
    dot_general x2 -> x0, matrix products: 6.65 us -> none  [the longest x1 4.28 us: shards(): jnp.dot(delta, passages, preferred_element_type=jnp.float32)]
  transfers between devices with their start and end apart: 1 -> 0, of which waited for: 1 -> 0; matrix products, arithmetic and copies ran while one was open for 0% -> 0% of each run, Pallas kernels for 0% -> 0%
where the time goes in v1:
time: 45.2 us; the launch traced here: 44.5 us
  Pallas kernels  39.2 us (87%)
  local copies, waits for them, and re-layouts  4.66 us (10%)
  between operations  0.65 us (1%)
    pallas_call x1, Pallas kernels, shards(): pl.pallas_call(functools.partial(kernel, stride, scale), out_shape=(jax.S...  39.2 us
    unnamed x10, local copies, waits for them, and re-layouts  4.66 us

profile of v1, /device:TPU:8, one launch (start us, length us, event | category | flops | bytes accessed | tf_op | source)
XLA Modules:
  0.0 44.5 jit_solution(6077608489809622520)
XLA Ops:
  0.6 0.0 copy-start
  0.6 1.4 %copy-done = bf16[1024,768]{1,0:T(8,128)(2,1)S(1)} copy-done((bf16[1024,768]{1,0:T(8,128)(2,1)S(1)}, bf16[1024,768]{1,0:T(8,128)(2,1)}, u32[]{:S(2)}) %copy-start) | copy-done | bytes 1572888
  2.0 0.0 copy-start.1
  2.0 0.7 %copy-done.1 = bf16[16,768]{1,0:T(8,128)(2,1)S(1)} copy-done((bf16[16,768]{1,0:T(8,128)(2,1)S(1)}, bf16[16,768]{1,0:T(8,128)(2,1)}, u32[]{:S(2)}) %copy-start.1) | copy-done | bytes 24600
  2.8 0.0 copy-start.2
  2.8 0.7 %copy-done.2 = s32[16,200]{1,0:T(8,128)S(1)} copy-done((s32[16,200]{1,0:T(8,128)S(1)}, s32[16,200]{1,0:T(8,128)}, u32[]{:S(2)}) %copy-start.2) | copy-done | bytes 12824
  3.5 0.0 copy-start.3
  3.5 0.7 %copy-done.3 = bf16[16,200]{1,0:T(8,128)(2,1)S(1)} copy-done((bf16[16,200]{1,0:T(8,128)(2,1)S(1)}, bf16[16,200]{1,0:T(8,128)(2,1)}, u32[]{:S(2)}) %copy-start.3) | copy-done | bytes 6424
  4.2 39.2 %shard_map.59 = (f32[1,16]{1,0:T(1,128)S(1)}, f32[2,768]{1,0:T(2,128)S(1)}) custom-call(bf16[16,768]{1,0:T(8,128)(2,1)S(1)} %copy-done.1, bf16[16,200]{1,0:T(8,128)(2,1)S(1)} %copy-done.3, s32[16,200]{1,0:T(8,128)S(1)} %copy-done.2, bf16[1024,768]{1,0:T(8,128)(2,1)S(1)} %copy-done), custom_call_target="tpu_custom_call" | custom-call | tf_op jit(solution)/shard_map/pallas_call | solution.py:383
  43.4 0.5 %copy.8 = f32[16]{0:T(128)} copy(f32[16]{0:T(128)S(1)} %bitcast.1) | data formatting | bytes 128
  43.9 0.6 %copy.9 = f32[2,768]{1,0:T(2,128)} copy(f32[2,768]{1,0:T(2,128)S(1)} %get-tuple-element.9) | data formatting | bytes 12288
Async XLA Ops:
  0.6 1.4 %copy-start = (bf16[1024,768]{1,0:T(8,128)(2,1)S(1)}, bf16[1024,768]{1,0:T(8,128)(2,1)}, u32[]{:S(2)}) copy-start(bf16[1024,768]{1,0:T(8,128)(2,1)} %pas_ref.1) | copy-start | bytes 4718596
  2.0 0.7 %copy-start.1 = (bf16[16,768]{1,0:T(8,128)(2,1)S(1)}, bf16[16,768]{1,0:T(8,128)(2,1)}, u32[]{:S(2)}) copy-start(bf16[16,768]{1,0:T(8,128)(2,1)} %q_ref.1) | copy-start | bytes 73732
  2.8 0.7 %copy-start.2 = (s32[16,200]{1,0:T(8,128)S(1)}, s32[16,200]{1,0:T(8,128)}, u32[]{:S(2)}) copy-start(s32[16,200]{1,0:T(8,128)} %id_ref.1) | copy-start | bytes 38404
  3.5 0.7 %copy-start.3 = (bf16[16,200]{1,0:T(8,128)(2,1)S(1)}, bf16[16,200]{1,0:T(8,128)(2,1)}, u32[]{:S(2)}) copy-start(bf16[16,200]{1,0:T(8,128)(2,1)} %w_ref.1) | copy-start | bytes 19204

commit v2 on v1

--- a/solution.py
+++ b/solution.py
@@ -42,12 +42,15 @@
 def kernel(
     stride,
     scale,
+    q_hbm,
+    w_hbm,
+    id_hbm,
+    pas_ref,
+    loss_ref,
+    grad_ref,
     q_ref,
     w_ref,
     id_ref,
-    pas_ref,
-    loss_ref,
-    grad_ref,
     pas,
     queries,
     cands,
@@ -63,6 +66,7 @@
     z_in,
     zstat_out,
     zstat_in,
+    in_sems,
     pas_sem,
     q_sems,
     c_sems,
@@ -106,8 +110,16 @@
     for target in greeted:
         pl.semaphore_signal(barrier, inc=1, device_id=target, device_id_type=MESH)
 
+    small = [
+        pltpu.make_async_copy(src, dst, in_sems.at[i])
+        for i, (src, dst) in enumerate(((w_hbm, w_ref), (id_hbm, id_ref), (q_hbm, q_ref)))
+    ]
+    for copy in small:
+        copy.start()
     load = pltpu.make_async_copy(pas_ref, pas.at[0], pas_sem.at[0])
     load.start()
+    for copy in small:
+        copy.wait()
 
     weights = w_ref[...].astype(F32)
     weight_sum = jnp.sum(weights, axis=1, keepdims=True)
@@ -309,15 +321,18 @@
 
     stacked = jnp.concatenate(
         [part[:, b * 128 : (b + 1) * 128] for part in (exp_rows, prob_rows) for b in range(6)], axis=0
-    ).astype(BF16)
-    o = iota((256, 1), 0)
-    j = o & 31
-    part = (j >= 12).astype(I32)
+    )
+    coarse = stacked.astype(BF16)
+    fine = (stacked - coarse.astype(F32)).astype(BF16)
+    stacked = jnp.concatenate([coarse, fine], axis=0)
+    o = iota((384, 1), 0)
+    d_of = o // 48
+    j = o - 48 * d_of
+    part = j // 12
     jj = j - 12 * part
-    source = part * 96 + (jj >> 1) * 16 + (o >> 5) * 2 + (jj & 1)
-    source = jnp.where(j < 24, source, -1)
-    order = (iota((256, 192), 1) == source).astype(F32).astype(BF16)
-    z_out[...] = jnp.dot(order, stacked, preferred_element_type=F32).astype(BF16).reshape(8, 32, 128)
+    source = part * 96 + (jj >> 1) * 16 + d_of * 2 + (jj & 1)
+    order = (iota((384, 384), 1) == source).astype(F32).astype(BF16)
+    z_out[...] = jnp.dot(order, stacked, preferred_element_type=F32).astype(BF16).reshape(8, 48, 128)
     z_copies = []
     for i, (target, d, slot) in enumerate(z_to):
         copy = pltpu.make_async_remote_copy(
@@ -361,6 +376,7 @@
     result = None
     for s in range(8):
         block = z_in[s].astype(F32)
+        block = block[0:24] + block[24:48]
         term = block[0:12] * columns[s][0:12] - block[12:24]
         result = term if result is None else result + term
     result = scale * result
@@ -382,10 +398,13 @@
     dma = pltpu.SemaphoreType.DMA
     loss, grad = pl.pallas_call(
         functools.partial(kernel, stride, scale),
-        out_shape=(jax.ShapeDtypeStruct((1, rows), F32), jax.ShapeDtypeStruct((2, depth), F32)),
-        in_specs=[vmem, vmem, vmem, pl.BlockSpec(memory_space=pl.ANY)],
+        out_shape=(pltpu.VMEM((1, rows), F32), pltpu.VMEM((2, depth), F32)),
+        in_specs=[pl.BlockSpec(memory_space=pltpu.HBM)] * 4,
         out_specs=(vmem, vmem),
         scratch_shapes=[
+            pltpu.VMEM((rows, depth), BF16),
+            pltpu.VMEM((rows, num_cand), BF16),
+            pltpu.VMEM((rows, num_cand), I32),
             pltpu.VMEM((2, width, depth), BF16),
             pltpu.VMEM((16, 16, depth), BF16),
             pltpu.VMEM((16, 16, 128), BF16),
@@ -397,10 +416,11 @@
             pltpu.VMEM((16, 16, depth), BF16),
             pltpu.VMEM((16, 16, depth), BF16),
             pltpu.VMEM((16, 8, 128), F32),
-            pltpu.VMEM((8, 32, 128), BF16),
-            pltpu.VMEM((8, 32, 128), BF16),
+            pltpu.VMEM((8, 48, 128), BF16),
+            pltpu.VMEM((8, 48, 128), BF16),
             pltpu.VMEM((8, 128), F32),
             pltpu.VMEM((8, 8, 128), F32),
+            dma((3,)),
             dma((3,)),
             dma((2, 15)),
             dma((2, 15)),
@@ -411,9 +431,9 @@
             dma((2, 7)),
         ],
         compiler_params=pltpu.CompilerParams(
-            collective_id=0, has_side_effects=True, vmem_limit_bytes=48 * 1024 * 1024
+            collective_id=0, has_side_effects=True, vmem_limit_bytes=60 * 1024 * 1024
         ),
-    )(queries, teacher_weight, cand_ids, passages)
+    )(*(pltpu.with_memory_space_constraint(a, pltpu.HBM) for a in (queries, teacher_weight, cand_ids, passages)))
     return (loss.reshape(rows), grad)
 
 

time: 45.2 us -> 42.2 us (0.934)
  local copies, waits for them, and re-layouts: 4.66 us -> 1.11 us
  Pallas kernels: 39.2 us -> 39.7 us
    unnamed x10 -> x2, local copies, waits for them, and re-layouts: 4.66 us -> 1.11 us
    pallas_call x1, Pallas kernels: 39.2 us -> 39.7 us  [shards(): pl.pallas_call(functools.partial(kernel, stride, scale), out_shape=(pltpu...]
where the time goes in v2:
time: 42.2 us; the launch traced here: 41.4 us
  Pallas kernels  39.7 us (94%)
  local copies, waits for them, and re-layouts  1.11 us (3%)
  between operations  0.64 us (2%)
    pallas_call x1, Pallas kernels, shards(): pl.pallas_call(functools.partial(kernel, stride, scale), out_shape=(pltpu...  39.7 us
    unnamed x2, local copies, waits for them, and re-layouts  1.11 us

profile of v2, /device:TPU:8, one launch (start us, length us, event | category | flops | bytes accessed | tf_op | source)
XLA Modules:
  0.0 41.4 jit_solution(6308269745938127534)
XLA Ops:
  0.6 39.7 %shard_map.59 = (f32[1,16]{1,0:T(1,128)S(1)}, f32[2,768]{1,0:T(2,128)S(1)}) custom-call(bf16[16,768]{1,0:T(8,128)(2,1)} %q_hbm.1, bf16[16,200]{1,0:T(8,128)(2,1)} %w_hbm.1, s32[16,200]{1,0:T(8,128)} %id_hbm.1, bf16[1024,768]{1,0:T(8,128)(2,1)} %pas_ref.1), custom_call_target="tpu_custom_call" | custom-call | tf_op jit(solution)/shard_map/pallas_call | solution.py:399
  40.3 0.5 %copy.8 = f32[16]{0:T(128)} copy(f32[16]{0:T(128)S(1)} %bitcast.1) | data formatting | bytes 128
  40.8 0.6 %copy.9 = f32[2,768]{1,0:T(2,128)} copy(f32[2,768]{1,0:T(2,128)S(1)} %get-tuple-element.7) | data formatting | bytes 12288

commit v3 on v2

--- a/solution.py
+++ b/solution.py
@@ -12,7 +12,9 @@
 F32 = jnp.float32
 BF16 = jnp.bfloat16
 I32 = jnp.int32
-FAR_FIRST = (4, 3, 5, 2, 6, 1, 7, 0)
+FAR_FIRST = (4, 3, 5, 2, 6, 1, 7)
+RELAYED = (1, 7, 2, 6)
+DIRECT = (4, 3, 5)
 
 
 def position():
@@ -84,29 +86,24 @@
     plane = width * 32
     per_plane = plane // stride
 
-    gather_to = [
-        (device(x, y if dy == 0 else 3 - y, (z + d) % 8, core), dy * 8 + (8 - d) % 8, d)
-        for d in FAR_FIRST
-        for dy in (0, 1)
-        if (d, dy) != (0, 0)
-    ]
     plane_to = [
         (
-            device((x + ex) % 4, (y + ey) % 4, z, core),
-            ex * 4 + ey,
-            ((4 - ex) % 4) * 4 + (4 - ey) % 4,
-            (((y + ey) % 4) // 2 + y_hi) % 2,
+            device((x + ex) % 4, ((y_hi + dy) % 2) * 2 + (y_lo + eyl) % 2, z, core),
+            dy * 8 + ex * 2 + eyl,
+            dy * 8 + ((4 - ex) % 4) * 2 + eyl,
         )
+        for dy in (0, 1)
         for ex in (2, 1, 3, 0)
-        for ey in (2, 1, 3, 0)
-        if (ex, ey) != (0, 0)
-    ]
-    z_to = [(device(x, y, (z + d) % 8, core), d, (8 - d) % 8) for d in FAR_FIRST if d]
+        for eyl in (0, 1)
+        if (dy, ex, eyl) != (0, 0, 0)
+    ]
+    z_to = [(device(x, y, (z + d) % 8, core), d, (8 - d) % 8) for d in FAR_FIRST]
     other = device(x, y, z, 1 - core)
 
     barrier = pltpu.get_barrier_semaphore()
-    greeted = [other] + [p[0] for p in plane_to]
-    greeted += [p[0] for p in gather_to if p[2] != 0]
+    greeted = [p[0] for p in plane_to] + [other]
+    greeted = [device(x, 3 - y, (z + d) % 8, core) for d in FAR_FIRST] + greeted
+    greeted = [p[0] for p in z_to] + greeted
     for target in greeted:
         pl.semaphore_signal(barrier, inc=1, device_id=target, device_id_type=MESH)
 
@@ -144,13 +141,12 @@
     cands[0] = cand_out[z]
     queries[0] = q_ref[...]
 
-    p_row = iota((256, 1), 0)
-    p_x = (x + (p_row >> 6)) & 3
-    p_y = (y + ((p_row >> 4) & 3)) & 3
-    p_dy = ((p_y >> 1) + y_hi) & 1
-    p_n = p_dy * 128 + ((p_row >> 1) & 7) * 16 + (p_x * 2 + (p_y & 1)) * 2 + (p_row & 1)
-    hot = (iota((256, 256), 1) == p_n).astype(F32)
-    perm_ref[...] = hot.astype(BF16)
+    p_row = iota((128, 1), 0)
+    p_x = (x + (p_row >> 5)) & 3
+    p_y = (y_lo + ((p_row >> 4) & 1)) & 1
+    p_n = ((p_row >> 1) & 7) * 16 + (p_x * 2 + p_y) * 2 + (p_row & 1)
+    mask = iota((128, 128), 1) == p_n
+    perm_ref[...] = mask.astype(F32).astype(BF16)
 
     pl.semaphore_wait(barrier, len(greeted))
 
@@ -159,30 +155,36 @@
     )
     swap.start()
     sent = []
-    cand_copies, q_copies = {}, {}
-    for i, (target, slot, d) in enumerate(gather_to):
+    mirror = device(x, 3 - y, z, core)
+
+    def send(src, dst, sems, i, target):
         copy = pltpu.make_async_remote_copy(
-            cand_out.at[(z + d) % 8],
-            cands.at[slot],
-            c_sems.at[0, i],
-            c_sems.at[1, i],
-            device_id=target,
-            device_id_type=MESH,
+            src, dst, sems.at[0, i], sems.at[1, i], device_id=target, device_id_type=MESH
         )
         copy.start()
-        cand_copies[i] = copy
-    for i, (target, slot, d) in enumerate(gather_to):
-        copy = pltpu.make_async_remote_copy(
-            q_ref,
-            queries.at[slot],
-            q_sems.at[0, i],
-            q_sems.at[1, i],
-            device_id=target,
-            device_id_type=MESH,
-        )
-        copy.start()
-        q_copies[i] = copy
-    sent += list(cand_copies.values()) + list(q_copies.values())
+        sent.append(copy)
+        return copy
+
+    cand_copies, near_copies, low_copies, high_copies = [], {}, [], []
+    for d in FAR_FIRST + (0,):
+        for dy in (0, 1):
+            if d or dy:
+                target = device(x, 3 - y if dy else y, (z + d) % 8, core)
+                slot = dy * 8 + (8 - d) % 8
+                cand_copies.append(send(cand_out.at[(z + d) % 8], cands.at[slot], c_sems, slot, target))
+    for d in RELAYED:
+        target = device(x, y, (z + d) % 8, core)
+        near_copies[d] = send(q_ref, queries.at[8 - d], q_sems, d, target)
+    for d in DIRECT:
+        target = device(x, y, (z + d) % 8, core)
+        low_copies.append(send(q_ref, queries.at[8 - d], q_sems, d, target))
+    for d in DIRECT:
+        target = device(x, 3 - y, (z + d) % 8, core)
+        high_copies.append(send(q_ref, queries.at[16 - d], q_sems, 8 + d, target))
+    high_copies.append(send(q_ref, queries.at[8], q_sems, 8, mirror))
+    for d in RELAYED:
+        near_copies[d].wait_recv()
+        high_copies.append(send(queries.at[8 - d], queries.at[16 - d], q_sems, 8 + d, mirror))
 
     offsets = [((((z * 2 + y_hi) * 2 + c) * 8) + slab) * width for c in (core, 1 - core)]
     firsts = [jnp.minimum(off // stride, num_cand - 2) - per_plane * z for off in offsets]
@@ -195,10 +197,16 @@
                     out_lane == (rho * 2 + c) * 3 + field, field * 32 + firsts[rho] + c, target_lane
                 )
     pick = (iota((128, 128), 0) == target_lane).astype(F32).astype(BF16)
-    for copy in cand_copies.values():
+    for copy in cand_copies:
         copy.wait_recv()
     picked = jnp.dot(cands[...].reshape(256, 128), pick, preferred_element_type=F32).astype(BF16)
-    picked = jnp.dot(perm_ref[...], picked, preferred_element_type=F32)
+    picked = jnp.concatenate(
+        [
+            jnp.dot(perm_ref[...], picked[h * 128 : h * 128 + 128], preferred_element_type=F32)
+            for h in range(2)
+        ],
+        axis=0,
+    )
     total_w = picked[:, 12:13] + picked[:, 13:14] + picked[:, 14:15]
     load.wait()
     column = iota((256, width), 1).astype(F32)
@@ -216,67 +224,42 @@
         part = jnp.dot(dense.astype(BF16), pas[rho], preferred_element_type=F32)
         prob_sum = part if prob_sum is None else prob_sum + part
     prob_out[...] = prob_sum.astype(BF16).reshape(16, 16, -1)
-    prob_copies = []
-    for i, (target, group, slot, _) in enumerate(plane_to):
-        copy = pltpu.make_async_remote_copy(
-            prob_out.at[group],
-            prob_in.at[slot],
-            prob_sems.at[0, i],
-            prob_sems.at[1, i],
-            device_id=target,
-            device_id_type=MESH,
+    prob_copies = [
+        send(prob_out.at[group], prob_in.at[slot], prob_sems, i, target)
+        for i, (target, group, slot) in enumerate(plane_to)
+    ]
+
+    depth = q_ref.shape[1]
+    nt = (((1,), (1,)), ((), ()))
+    exp_copies, stat_copies = [], []
+    for h, waits in enumerate((low_copies, high_copies)):
+        for copy in waits:
+            copy.wait_recv()
+        half = queries[h * 8 : h * 8 + 8].reshape(128, depth)
+        rows = jnp.dot(perm_ref[...], half, preferred_element_type=F32)
+        rows16 = rows.astype(BF16)
+        scores = [
+            scale * lax.dot_general(rows16, pas[rho], nt, preferred_element_type=F32)
+            for rho in range(2)
+        ]
+        peak = jnp.maximum(
+            jnp.max(scores[0], axis=1, keepdims=True), jnp.max(scores[1], axis=1, keepdims=True)
         )
-        copy.start()
-        prob_copies.append(copy)
-    sent += prob_copies
-
-    for copy in q_copies.values():
-        copy.wait_recv()
-    depth = q_ref.shape[1]
-    rows = jnp.dot(perm_ref[...], queries[...].reshape(256, depth), preferred_element_type=F32)
-    rows16 = rows.astype(BF16)
-    teacher = scale * jnp.sum(rows * prob_sum, axis=1, keepdims=True)
-    nt = (((1,), (1,)), ((), ()))
-    scores = [
-        scale * lax.dot_general(rows16, pas[rho], nt, preferred_element_type=F32) for rho in range(2)
-    ]
-    peak = jnp.maximum(
-        jnp.max(scores[0], axis=1, keepdims=True), jnp.max(scores[1], axis=1, keepdims=True)
-    )
-    exps = [jnp.exp(s - peak) for s in scores]
-    total = jnp.sum(exps[0], axis=1, keepdims=True) + jnp.sum(exps[1], axis=1, keepdims=True)
-    mixed = jnp.dot(exps[0].astype(BF16), pas[0], preferred_element_type=F32) + jnp.dot(
-        exps[1].astype(BF16), pas[1], preferred_element_type=F32
-    )
-    exp_out[...] = mixed.astype(BF16).reshape(16, 16, depth)
-    mask = perm_ref[...].astype(F32) > 0.5
-    for k, stat in enumerate((peak, total, teacher)):
-        lanes = jnp.sum(jnp.where(mask, stat, 0.0), axis=0, keepdims=True)
-        stat_out[0, k : k + 1, :] = lanes[:, :128]
-        stat_out[1, k : k + 1, :] = lanes[:, 128:]
-    exp_copies, stat_copies = [], []
-    for i, (target, group, slot, dy) in enumerate(plane_to):
-        copy = pltpu.make_async_remote_copy(
-            stat_out.at[dy],
-            stat_in.at[slot],
-            stat_sems.at[0, i],
-            stat_sems.at[1, i],
-            device_id=target,
-            device_id_type=MESH,
+        exps = [jnp.exp(s - peak) for s in scores]
+        mixed = jnp.dot(exps[0].astype(BF16), pas[0], preferred_element_type=F32) + jnp.dot(
+            exps[1].astype(BF16), pas[1], preferred_element_type=F32
         )
-        copy.start()
-        stat_copies.append(copy)
-        copy = pltpu.make_async_remote_copy(
-            exp_out.at[group],
-            exp_in.at[slot],
-            exp_sems.at[0, i],
-            exp_sems.at[1, i],
-            device_id=target,
-            device_id_type=MESH,
-        )
-        copy.start()
-        exp_copies.append(copy)
-    sent += exp_copies + stat_copies
+        exp_out[h * 8 : h * 8 + 8] = mixed.astype(BF16).reshape(8, 16, depth)
+        for i, (target, group, slot) in enumerate(plane_to):
+            if group // 8 == h:
+                exp_copies.append(send(exp_out.at[group], exp_in.at[slot], exp_sems, i, target))
+        total = jnp.sum(exps[0], axis=1, keepdims=True) + jnp.sum(exps[1], axis=1, keepdims=True)
+        teacher = scale * jnp.sum(rows * prob_sum[h * 128 : h * 128 + 128], axis=1, keepdims=True)
+        for k, stat in enumerate((peak, total, teacher)):
+            stat_out[h, k : k + 1, :] = jnp.sum(jnp.where(mask, stat, 0.0), axis=0, keepdims=True)
+        for i, (target, group, slot) in enumerate(plane_to):
+            if group // 8 == h:
+                stat_copies.append(send(stat_out.at[h], stat_in.at[slot], stat_sems, i, target))
 
     stat_in[0] = stat_out[0]
     for copy in prob_copies:
@@ -296,18 +279,10 @@
     zstat_out[0:1, :] = peak
     zstat_out[1:2, :] = total
     zstat_out[2:3, :] = teacher
-    zstat_copies = []
-    for i, (target, d, slot) in enumerate(z_to):
-        copy = pltpu.make_async_remote_copy(
-            zstat_out,
-            zstat_in.at[slot],
-            zstat_sems.at[0, i],
-            zstat_sems.at[1, i],
-            device_id=target,
-            device_id_type=MESH,
-        )
-        copy.start()
-        zstat_copies.append(copy)
+    zstat_copies = [
+        send(zstat_out, zstat_in.at[slot], zstat_sems, i, target)
+        for i, (target, d, slot) in enumerate(z_to)
+    ]
     row = iota((16, 128), 0)
     own_lane = iota((16, 128), 1) == (row >> 1) * 16 + slab * 2 + (row & 1)
     columns = [
@@ -333,19 +308,9 @@
     source = part * 96 + (jj >> 1) * 16 + d_of * 2 + (jj & 1)
     order = (iota((384, 384), 1) == source).astype(F32).astype(BF16)
     z_out[...] = jnp.dot(order, stacked, preferred_element_type=F32).astype(BF16).reshape(8, 48, 128)
-    z_copies = []
-    for i, (target, d, slot) in enumerate(z_to):
-        copy = pltpu.make_async_remote_copy(
-            z_out.at[d],
-            z_in.at[slot],
-            z_sems.at[0, i],
-            z_sems.at[1, i],
-            device_id=target,
-            device_id_type=MESH,
-        )
-        copy.start()
-        z_copies.append(copy)
-    sent += zstat_copies + z_copies
+    z_copies = [
+        send(z_out.at[d], z_in.at[slot], z_sems, i, target) for i, (target, d, slot) in enumerate(z_to)
+    ]
 
     zstat_in[0] = zstat_out[...]
     entropy_lanes = jnp.sum(
@@ -409,7 +374,7 @@
             pltpu.VMEM((16, 16, depth), BF16),
             pltpu.VMEM((16, 16, 128), BF16),
             pltpu.VMEM((8, 16, 128), BF16),
-            pltpu.VMEM((256, 256), BF16),
+            pltpu.VMEM((128, 128), BF16),
             pltpu.VMEM((16, 16, depth), BF16),
             pltpu.VMEM((16, 16, depth), BF16),
             pltpu.VMEM((2, 8, 128), F32),
@@ -422,8 +387,8 @@
             pltpu.VMEM((8, 8, 128), F32),
             dma((3,)),
             dma((3,)),
-            dma((2, 15)),
-            dma((2, 15)),
+            dma((2, 16)),
+            dma((2, 16)),
             dma((2, 15)),
             dma((2, 15)),
             dma((2, 15)),

time: 42.2 us -> 39.6 us (0.938)
  Pallas kernels: 39.7 us -> 37.5 us
    pallas_call x1, Pallas kernels: 39.7 us -> 37.5 us  [shards(): pl.pallas_call(functools.partial(kernel, stride, scale), out_shape=(pltpu...]
where the time goes in v3:
time: 39.6 us; the launch traced here: 39.3 us
  Pallas kernels  37.5 us (95%)
  local copies, waits for them, and re-layouts  1.11 us (3%)
  between operations  0.64 us (2%)
    pallas_call x1, Pallas kernels, shards(): pl.pallas_call(functools.partial(kernel, stride, scale), out_shape=(pltpu...  37.5 us
    unnamed x2, local copies, waits for them, and re-layouts  1.11 us

profile of v3, /device:TPU:8, one launch (start us, length us, event | category | flops | bytes accessed | tf_op | source)
XLA Modules:
  0.0 39.3 jit_solution(8292667404088242766)
XLA Ops:
  0.6 37.5 %shard_map.59 = (f32[1,16]{1,0:T(1,128)S(1)}, f32[2,768]{1,0:T(2,128)S(1)}) custom-call(bf16[16,768]{1,0:T(8,128)(2,1)} %q_hbm.1, bf16[16,200]{1,0:T(8,128)(2,1)} %w_hbm.1, s32[16,200]{1,0:T(8,128)} %id_hbm.1, bf16[1024,768]{1,0:T(8,128)(2,1)} %pas_ref.1), custom_call_target="tpu_custom_call" | custom-call | tf_op jit(solution)/shard_map/pallas_call | solution.py:364
  38.1 0.5 %copy.8 = f32[16]{0:T(128)} copy(f32[16]{0:T(128)S(1)} %bitcast.1) | data formatting | bytes 128
  38.7 0.6 %copy.9 = f32[2,768]{1,0:T(2,128)} copy(f32[2,768]{1,0:T(2,128)S(1)} %get-tuple-element.7) | data formatting | bytes 12288

commit v4 on v3

--- a/solution.py
+++ b/solution.py
@@ -54,6 +54,7 @@
     w_ref,
     id_ref,
     pas,
+    pas_t,
     queries,
     cands,
     cand_out,
@@ -62,6 +63,8 @@
     exp_out,
     stat_out,
     prob_in,
+    line_out,
+    line_in,
     exp_in,
     stat_in,
     z_out,
@@ -141,13 +144,6 @@
     cands[0] = cand_out[z]
     queries[0] = q_ref[...]
 
-    p_row = iota((128, 1), 0)
-    p_x = (x + (p_row >> 5)) & 3
-    p_y = (y_lo + ((p_row >> 4) & 1)) & 1
-    p_n = ((p_row >> 1) & 7) * 16 + (p_x * 2 + p_y) * 2 + (p_row & 1)
-    mask = iota((128, 128), 1) == p_n
-    perm_ref[...] = mask.astype(F32).astype(BF16)
-
     pl.semaphore_wait(barrier, len(greeted))
 
     swap = pltpu.make_async_remote_copy(
@@ -182,9 +178,12 @@
         target = device(x, 3 - y, (z + d) % 8, core)
         high_copies.append(send(q_ref, queries.at[16 - d], q_sems, 8 + d, target))
     high_copies.append(send(q_ref, queries.at[8], q_sems, 8, mirror))
-    for d in RELAYED:
-        near_copies[d].wait_recv()
-        high_copies.append(send(queries.at[8 - d], queries.at[16 - d], q_sems, 8 + d, mirror))
+    p_row = iota((128, 1), 0)
+    p_x = (x + (p_row >> 5)) & 3
+    p_y = (y_lo + ((p_row >> 4) & 1)) & 1
+    p_n = ((p_row >> 1) & 7) * 16 + (p_x * 2 + p_y) * 2 + (p_row & 1)
+    mask = iota((128, 128), 1) == p_n
+    perm_ref[...] = mask.astype(F32).astype(BF16)
 
     offsets = [((((z * 2 + y_hi) * 2 + c) * 8) + slab) * width for c in (core, 1 - core)]
     firsts = [jnp.minimum(off // stride, num_cand - 2) - per_plane * z for off in offsets]
@@ -197,6 +196,15 @@
                     out_lane == (rho * 2 + c) * 3 + field, field * 32 + firsts[rho] + c, target_lane
                 )
     pick = (iota((128, 128), 0) == target_lane).astype(F32).astype(BF16)
+    load.wait()
+    pas_t[0] = pas[0].T
+    for d in RELAYED:
+        near_copies[d].wait_recv()
+        high_copies.append(send(queries.at[8 - d], queries.at[16 - d], q_sems, 8 + d, mirror))
+
+    swap.wait_recv()
+    pas_t[1] = pas[1].T
+
     for copy in cand_copies:
         copy.wait_recv()
     picked = jnp.dot(cands[...].reshape(256, 128), pick, preferred_element_type=F32).astype(BF16)
@@ -208,10 +216,8 @@
         axis=0,
     )
     total_w = picked[:, 12:13] + picked[:, 13:14] + picked[:, 14:15]
-    load.wait()
     column = iota((256, width), 1).astype(F32)
     prob_sum = None
-    swap.wait_recv()
     for rho in range(2):
         shift = (per_plane * stride * z - offsets[rho]).astype(F32)
         dense = None
@@ -223,14 +229,16 @@
             dense = term if dense is None else dense + term
         part = jnp.dot(dense.astype(BF16), pas[rho], preferred_element_type=F32)
         prob_sum = part if prob_sum is None else prob_sum + part
-    prob_out[...] = prob_sum.astype(BF16).reshape(16, 16, -1)
+    groups = prob_sum.astype(BF16).reshape(2, 4, 2, 16, -1)
+    for dy in range(2):
+        for ex in range(4):
+            prob_out[ex, dy * 2 : dy * 2 + 2] = groups[dy, ex]
     prob_copies = [
-        send(prob_out.at[group], prob_in.at[slot], prob_sems, i, target)
-        for i, (target, group, slot) in enumerate(plane_to)
+        send(prob_out.at[ex], prob_in.at[4 - ex], prob_sems, ex, device((x + ex) % 4, y, z, core))
+        for ex in (2, 1, 3)
     ]
 
     depth = q_ref.shape[1]
-    nt = (((1,), (1,)), ((), ()))
     exp_copies, stat_copies = [], []
     for h, waits in enumerate((low_copies, high_copies)):
         for copy in waits:
@@ -239,7 +247,7 @@
         rows = jnp.dot(perm_ref[...], half, preferred_element_type=F32)
         rows16 = rows.astype(BF16)
         scores = [
-            scale * lax.dot_general(rows16, pas[rho], nt, preferred_element_type=F32)
+            scale * jnp.dot(rows16, pas_t[rho], preferred_element_type=F32)
             for rho in range(2)
         ]
         peak = jnp.maximum(
@@ -262,11 +270,27 @@
                 stat_copies.append(send(stat_out.at[h], stat_in.at[slot], stat_sems, i, target))
 
     stat_in[0] = stat_out[0]
+    o = iota((384, 1), 0)
+    d_of = o // 48
+    j = o - 48 * d_of
+    part = j // 12
+    jj = j - 12 * part
+    source = part * 96 + (jj >> 1) * 16 + d_of * 2 + (jj & 1)
+    order = (iota((384, 384), 1) == source).astype(F32).astype(BF16)
+    entropy_lanes = jnp.sum(
+        jnp.where(iota((16, 16), 0) == iota((16, 16), 1), entropy, 0.0), axis=0, keepdims=True
+    )
     for copy in prob_copies:
         copy.wait_recv()
     prob_rows = prob_out[0].astype(F32)
-    for i in range(1, 16):
+    for i in range(1, 4):
         prob_rows = prob_rows + prob_in[i].astype(F32)
+    line_out[...] = prob_rows.astype(BF16)
+    prob_rows = prob_rows[0]
+    line_copies = []
+    for k in (2, 3, 1):
+        target = device(x, ((y_hi + k // 2) % 2) * 2 + (y_lo + k % 2) % 2, z, core)
+        line_copies.append(send(line_out.at[k], line_in.at[k], prob_sems, 3 + k, target))
     for copy in stat_copies:
         copy.wait_recv()
     peaks = jnp.concatenate([stat_in[i, 0:1, :] for i in range(16)], axis=0)
@@ -288,11 +312,15 @@
     columns = [
         jnp.sum(jnp.where(own_lane, share[i : i + 1, :], 0.0), axis=1, keepdims=True) for i in range(16)
     ]
-    for copy in exp_copies:
-        copy.wait_recv()
     exp_rows = exp_out[0].astype(F32) * columns[0]
-    for i in range(1, 16):
-        exp_rows = exp_rows + exp_in[i].astype(F32) * columns[i]
+    for copy, (_, _, slot) in zip(exp_copies, plane_to):
+        copy.wait_recv()
+        exp_rows = exp_rows + exp_in[slot].astype(F32) * columns[slot]
+
+    for copy in line_copies:
+        copy.wait_recv()
+    for k in range(1, 4):
+        prob_rows = prob_rows + line_in[k].astype(F32)
 
     stacked = jnp.concatenate(
         [part[:, b * 128 : (b + 1) * 128] for part in (exp_rows, prob_rows) for b in range(6)], axis=0
@@ -300,22 +328,12 @@
     coarse = stacked.astype(BF16)
     fine = (stacked - coarse.astype(F32)).astype(BF16)
     stacked = jnp.concatenate([coarse, fine], axis=0)
-    o = iota((384, 1), 0)
-    d_of = o // 48
-    j = o - 48 * d_of
-    part = j // 12
-    jj = j - 12 * part
-    source = part * 96 + (jj >> 1) * 16 + d_of * 2 + (jj & 1)
-    order = (iota((384, 384), 1) == source).astype(F32).astype(BF16)
     z_out[...] = jnp.dot(order, stacked, preferred_element_type=F32).astype(BF16).reshape(8, 48, 128)
     z_copies = [
         send(z_out.at[d], z_in.at[slot], z_sems, i, target) for i, (target, d, slot) in enumerate(z_to)
     ]
 
     zstat_in[0] = zstat_out[...]
-    entropy_lanes = jnp.sum(
-        jnp.where(iota((16, 16), 0) == iota((16, 16), 1), entropy, 0.0), axis=0, keepdims=True
-    )
     for copy in zstat_copies:
         copy.wait_recv()
 
@@ -371,14 +389,17 @@
             pltpu.VMEM((rows, num_cand), BF16),
             pltpu.VMEM((rows, num_cand), I32),
             pltpu.VMEM((2, width, depth), BF16),
+            pltpu.VMEM((2, depth, width), BF16),
             pltpu.VMEM((16, 16, depth), BF16),
             pltpu.VMEM((16, 16, 128), BF16),
             pltpu.VMEM((8, 16, 128), BF16),
             pltpu.VMEM((128, 128), BF16),
-            pltpu.VMEM((16, 16, depth), BF16),
+            pltpu.VMEM((4, 4, 16, depth), BF16),
             pltpu.VMEM((16, 16, depth), BF16),
             pltpu.VMEM((2, 8, 128), F32),
-            pltpu.VMEM((16, 16, depth), BF16),
+            pltpu.VMEM((4, 4, 16, depth), BF16),
+            pltpu.VMEM((4, 16, depth), BF16),
+            pltpu.VMEM((4, 16, depth), BF16),
             pltpu.VMEM((16, 16, depth), BF16),
             pltpu.VMEM((16, 8, 128), F32),
             pltpu.VMEM((8, 48, 128), BF16),

time: 39.6 us -> 39.2 us (0.990)
  Pallas kernels: 37.5 us -> 37 us
    pallas_call x1, Pallas kernels: 37.5 us -> 37 us  [shards(): pl.pallas_call(functools.partial(kernel, stride, scale), out_shape=(pltpu...]
where the time goes in v4:
time: 39.2 us; the launch traced here: 38.8 us
  Pallas kernels  37 us (94%)
  local copies, waits for them, and re-layouts  1.11 us (3%)
  between operations  0.64 us (2%)
    pallas_call x1, Pallas kernels, shards(): pl.pallas_call(functools.partial(kernel, stride, scale), out_shape=(pltpu...  37 us
    unnamed x2, local copies, waits for them, and re-layouts  1.11 us

profile of v4, /device:TPU:8, one launch (start us, length us, event | category | flops | bytes accessed | tf_op | source)
XLA Modules:
  0.0 38.8 jit_solution(17551556672699371597)
XLA Ops:
  0.6 37.0 %shard_map.59 = (f32[1,16]{1,0:T(1,128)S(1)}, f32[2,768]{1,0:T(2,128)S(1)}) custom-call(bf16[16,768]{1,0:T(8,128)(2,1)} %q_hbm.1, bf16[16,200]{1,0:T(8,128)(2,1)} %w_hbm.1, s32[16,200]{1,0:T(8,128)} %id_hbm.1, bf16[1024,768]{1,0:T(8,128)(2,1)} %pas_ref.1), custom_call_target="tpu_custom_call" | custom-call | tf_op jit(solution)/shard_map/pallas_call | solution.py:382
  37.7 0.5 %copy.8 = f32[16]{0:T(128)} copy(f32[16]{0:T(128)S(1)} %bitcast.1) | data formatting | bytes 128
  38.2 0.6 %copy.9 = f32[2,768]{1,0:T(2,128)} copy(f32[2,768]{1,0:T(2,128)S(1)} %get-tuple-element.7) | data formatting | bytes 12288

commit v5 on v4

--- a/solution.py
+++ b/solution.py
@@ -198,13 +198,6 @@
     pick = (iota((128, 128), 0) == target_lane).astype(F32).astype(BF16)
     load.wait()
     pas_t[0] = pas[0].T
-    for d in RELAYED:
-        near_copies[d].wait_recv()
-        high_copies.append(send(queries.at[8 - d], queries.at[16 - d], q_sems, 8 + d, mirror))
-
-    swap.wait_recv()
-    pas_t[1] = pas[1].T
-
     for copy in cand_copies:
         copy.wait_recv()
     picked = jnp.dot(cands[...].reshape(256, 128), pick, preferred_element_type=F32).astype(BF16)
@@ -216,27 +209,38 @@
         axis=0,
     )
     total_w = picked[:, 12:13] + picked[:, 13:14] + picked[:, 14:15]
-    column = iota((256, width), 1).astype(F32)
-    prob_sum = None
-    for rho in range(2):
-        shift = (per_plane * stride * z - offsets[rho]).astype(F32)
-        dense = None
-        for c in range(2):
-            at = (rho * 2 + c) * 3
-            local = picked[:, at : at + 1] * 256.0 + picked[:, at + 1 : at + 2] + shift
-            prob = picked[:, at + 2 : at + 3] / total_w
-            term = jnp.where(column == local, prob, 0.0)
-            dense = term if dense is None else dense + term
-        part = jnp.dot(dense.astype(BF16), pas[rho], preferred_element_type=F32)
-        prob_sum = part if prob_sum is None else prob_sum + part
-    groups = prob_sum.astype(BF16).reshape(2, 4, 2, 16, -1)
-    for dy in range(2):
-        for ex in range(4):
-            prob_out[ex, dy * 2 : dy * 2 + 2] = groups[dy, ex]
-    prob_copies = [
-        send(prob_out.at[ex], prob_in.at[4 - ex], prob_sems, ex, device((x + ex) % 4, y, z, core))
-        for ex in (2, 1, 3)
-    ]
+    for d in RELAYED:
+        near_copies[d].wait_recv()
+        high_copies.append(send(queries.at[8 - d], queries.at[16 - d], q_sems, 8 + d, mirror))
+
+    swap.wait_recv()
+    pas_t[1] = pas[1].T
+
+    column = iota((128, width), 1).astype(F32)
+    prob_copies, prob_sums = [], []
+    for h in range(2):
+        mine = slice(h * 128, h * 128 + 128)
+        prob_sum = None
+        for rho in range(2):
+            shift = (per_plane * stride * z - offsets[rho]).astype(F32)
+            dense = 0.0
+            for c in range(2):
+                at = (rho * 2 + c) * 3
+                local = picked[mine, at : at + 1] * 256.0 + picked[mine, at + 1 : at + 2] + shift
+                prob = picked[mine, at + 2 : at + 3] / total_w[mine]
+                dense = jnp.where(column == local, prob, dense)
+            part = jnp.dot(dense.astype(BF16), pas[rho], preferred_element_type=F32)
+            prob_sum = part if prob_sum is None else prob_sum + part
+        prob_sums.append(prob_sum)
+        groups = prob_sum.astype(BF16).reshape(4, 2, 16, -1)
+        span = pl.ds(h * 2, 2)
+        for ex in (2, 1, 3, 0):
+            prob_out[ex, span] = groups[ex]
+            if ex:
+                target = device((x + ex) % 4, y, z, core)
+                prob_copies.append(
+                    send(prob_out.at[ex, span], prob_in.at[4 - ex, span], prob_sems, ex + 4 * h, target)
+                )
 
     depth = q_ref.shape[1]
     exp_copies, stat_copies = [], []
@@ -262,7 +266,7 @@
             if group // 8 == h:
                 exp_copies.append(send(exp_out.at[group], exp_in.at[slot], exp_sems, i, target))
         total = jnp.sum(exps[0], axis=1, keepdims=True) + jnp.sum(exps[1], axis=1, keepdims=True)
-        teacher = scale * jnp.sum(rows * prob_sum[h * 128 : h * 128 + 128], axis=1, keepdims=True)
+        teacher = scale * jnp.sum(rows * prob_sums[h], axis=1, keepdims=True)
         for k, stat in enumerate((peak, total, teacher)):
             stat_out[h, k : k + 1, :] = jnp.sum(jnp.where(mask, stat, 0.0), axis=0, keepdims=True)
         for i, (target, group, slot) in enumerate(plane_to):
@@ -290,7 +294,7 @@
     line_copies = []
     for k in (2, 3, 1):
         target = device(x, ((y_hi + k // 2) % 2) * 2 + (y_lo + k % 2) % 2, z, core)
-        line_copies.append(send(line_out.at[k], line_in.at[k], prob_sems, 3 + k, target))
+        line_copies.append(send(line_out.at[k], line_in.at[k], prob_sems, 7 + k, target))
     for copy in stat_copies:
         copy.wait_recv()
     peaks = jnp.concatenate([stat_in[i, 0:1, :] for i in range(16)], axis=0)

time: 39.2 us -> 38.6 us (0.985)
  Pallas kernels: 37 us -> 36.6 us
    pallas_call x1, Pallas kernels: 37 us -> 36.6 us  [shards(): pl.pallas_call(functools.partial(kernel, stride, scale), out_shape=(pltpu...]
where the time goes in v5:
time: 38.6 us; the launch traced here: 38.4 us
  Pallas kernels  36.6 us (95%)
  local copies, waits for them, and re-layouts  1.11 us (3%)
  between operations  0.64 us (2%)
    pallas_call x1, Pallas kernels, shards(): pl.pallas_call(functools.partial(kernel, stride, scale), out_shape=(pltpu...  36.6 us
    unnamed x2, local copies, waits for them, and re-layouts  1.11 us

profile of v5, /device:TPU:8, one launch (start us, length us, event | category | flops | bytes accessed | tf_op | source)
XLA Modules:
  0.0 38.4 jit_solution(12652401130789858700)
XLA Ops:
  0.6 36.6 %shard_map.59 = (f32[1,16]{1,0:T(1,128)S(1)}, f32[2,768]{1,0:T(2,128)S(1)}) custom-call(bf16[16,768]{1,0:T(8,128)(2,1)} %q_hbm.1, bf16[16,200]{1,0:T(8,128)(2,1)} %w_hbm.1, s32[16,200]{1,0:T(8,128)} %id_hbm.1, bf16[1024,768]{1,0:T(8,128)(2,1)} %pas_ref.1), custom_call_target="tpu_custom_call" | custom-call | tf_op jit(solution)/shard_map/pallas_call | solution.py:386
  37.3 0.5 %copy.8 = f32[16]{0:T(128)} copy(f32[16]{0:T(128)S(1)} %bitcast.1) | data formatting | bytes 128
  37.8 0.6 %copy.9 = f32[2,768]{1,0:T(2,128)} copy(f32[2,768]{1,0:T(2,128)S(1)} %get-tuple-element.7) | data formatting | bytes 12288

commit v6 on v5

--- a/solution.py
+++ b/solution.py
@@ -13,8 +13,8 @@
 BF16 = jnp.bfloat16
 I32 = jnp.int32
 FAR_FIRST = (4, 3, 5, 2, 6, 1, 7)
-RELAYED = (1, 7, 2, 6)
-DIRECT = (4, 3, 5)
+RELAYED = (2, 6)
+DIRECT = (4, 3, 5, 1, 7)
 
 
 def position():
@@ -172,12 +172,12 @@
         target = device(x, y, (z + d) % 8, core)
         near_copies[d] = send(q_ref, queries.at[8 - d], q_sems, d, target)
     for d in DIRECT:
-        target = device(x, y, (z + d) % 8, core)
-        low_copies.append(send(q_ref, queries.at[8 - d], q_sems, d, target))
-    for d in DIRECT:
         target = device(x, 3 - y, (z + d) % 8, core)
         high_copies.append(send(q_ref, queries.at[16 - d], q_sems, 8 + d, target))
     high_copies.append(send(q_ref, queries.at[8], q_sems, 8, mirror))
+    for d in DIRECT:
+        target = device(x, y, (z + d) % 8, core)
+        low_copies.append(send(q_ref, queries.at[8 - d], q_sems, d, target))
     p_row = iota((128, 1), 0)
     p_x = (x + (p_row >> 5)) & 3
     p_y = (y_lo + ((p_row >> 4) & 1)) & 1
@@ -244,7 +244,7 @@
 
     depth = q_ref.shape[1]
     exp_copies, stat_copies = [], []
-    for h, waits in enumerate((low_copies, high_copies)):
+    for h, waits in ((1, high_copies), (0, low_copies)):
         for copy in waits:
             copy.wait_recv()
         half = queries[h * 8 : h * 8 + 8].reshape(128, depth)
@@ -317,7 +317,7 @@
         jnp.sum(jnp.where(own_lane, share[i : i + 1, :], 0.0), axis=1, keepdims=True) for i in range(16)
     ]
     exp_rows = exp_out[0].astype(F32) * columns[0]
-    for copy, (_, _, slot) in zip(exp_copies, plane_to):
+    for copy, (_, _, slot) in zip(exp_copies, plane_to[7:] + plane_to[:7]):
         copy.wait_recv()
         exp_rows = exp_rows + exp_in[slot].astype(F32) * columns[slot]
 

time: 38.6 us -> 38.1 us (0.987)
  Pallas kernels: 36.6 us -> 36.2 us
    pallas_call x1, Pallas kernels: 36.6 us -> 36.2 us  [shards(): pl.pallas_call(functools.partial(kernel, stride, scale), out_shape=(pltpu...]
where the time goes in v6:
time: 38.1 us; the launch traced here: 38 us
  Pallas kernels  36.2 us (95%)
  local copies, waits for them, and re-layouts  1.11 us (3%)
  between operations  0.64 us (2%)
    pallas_call x1, Pallas kernels, shards(): pl.pallas_call(functools.partial(kernel, stride, scale), out_shape=(pltpu...  36.2 us
    unnamed x2, local copies, waits for them, and re-layouts  1.11 us

profile of v6, /device:TPU:8, one launch (start us, length us, event | category | flops | bytes accessed | tf_op | source)
XLA Modules:
  0.0 38.0 jit_solution(6255010384206065907)
XLA Ops:
  0.6 36.2 %shard_map.59 = (f32[1,16]{1,0:T(1,128)S(1)}, f32[2,768]{1,0:T(2,128)S(1)}) custom-call(bf16[16,768]{1,0:T(8,128)(2,1)} %q_hbm.1, bf16[16,200]{1,0:T(8,128)(2,1)} %w_hbm.1, s32[16,200]{1,0:T(8,128)} %id_hbm.1, bf16[1024,768]{1,0:T(8,128)(2,1)} %pas_ref.1), custom_call_target="tpu_custom_call" | custom-call | tf_op jit(solution)/shard_map/pallas_call | solution.py:386
  36.9 0.5 %copy.8 = f32[16]{0:T(128)} copy(f32[16]{0:T(128)S(1)} %bitcast.1) | data formatting | bytes 128
  37.4 0.6 %copy.9 = f32[2,768]{1,0:T(2,128)} copy(f32[2,768]{1,0:T(2,128)S(1)} %get-tuple-element.7) | data formatting | bytes 12288

commit v7 on v6

--- a/solution.py
+++ b/solution.py
@@ -14,7 +14,7 @@
 I32 = jnp.int32
 FAR_FIRST = (4, 3, 5, 2, 6, 1, 7)
 RELAYED = (2, 6)
-DIRECT = (4, 3, 5, 1, 7)
+DIRECT = (1, 7, 4, 3, 5)
 
 
 def position():
@@ -97,7 +97,7 @@
         )
         for dy in (0, 1)
         for ex in (2, 1, 3, 0)
-        for eyl in (0, 1)
+        for eyl in (1, 0)
         if (dy, ex, eyl) != (0, 0, 0)
     ]
     z_to = [(device(x, y, (z + d) % 8, core), d, (8 - d) % 8) for d in FAR_FIRST]
@@ -217,8 +217,8 @@
     pas_t[1] = pas[1].T
 
     column = iota((128, width), 1).astype(F32)
-    prob_copies, prob_sums = [], []
-    for h in range(2):
+    prob_copies, prob_sums = [], {}
+    for h in (1, 0):
         mine = slice(h * 128, h * 128 + 128)
         prob_sum = None
         for rho in range(2):
@@ -231,7 +231,7 @@
                 dense = jnp.where(column == local, prob, dense)
             part = jnp.dot(dense.astype(BF16), pas[rho], preferred_element_type=F32)
             prob_sum = part if prob_sum is None else prob_sum + part
-        prob_sums.append(prob_sum)
+        prob_sums[h] = prob_sum
         groups = prob_sum.astype(BF16).reshape(4, 2, 16, -1)
         span = pl.ds(h * 2, 2)
         for ex in (2, 1, 3, 0):

time: 38.1 us -> 38.1 us (level)
  no operation moved by 1% of the time
where the time goes in v7:
time: 38.1 us; the launch traced here: 37.9 us
  Pallas kernels  36.1 us (95%)
  local copies, waits for them, and re-layouts  1.11 us (3%)
  between operations  0.64 us (2%)
    pallas_call x1, Pallas kernels, shards(): pl.pallas_call(functools.partial(kernel, stride, scale), out_shape=(pltpu...  36.1 us
    unnamed x2, local copies, waits for them, and re-layouts  1.11 us

profile of v7, /device:TPU:8, one launch (start us, length us, event | category | flops | bytes accessed | tf_op | source)
XLA Modules:
  0.0 37.9 jit_solution(16750632843731232040)
XLA Ops:
  0.6 36.1 %shard_map.59 = (f32[1,16]{1,0:T(1,128)S(1)}, f32[2,768]{1,0:T(2,128)S(1)}) custom-call(bf16[16,768]{1,0:T(8,128)(2,1)} %q_hbm.1, bf16[16,200]{1,0:T(8,128)(2,1)} %w_hbm.1, s32[16,200]{1,0:T(8,128)} %id_hbm.1, bf16[1024,768]{1,0:T(8,128)(2,1)} %pas_ref.1), custom_call_target="tpu_custom_call" | custom-call | tf_op jit(solution)/shard_map/pallas_call | solution.py:386
  36.8 0.5 %copy.8 = f32[16]{0:T(128)} copy(f32[16]{0:T(128)S(1)} %bitcast.1) | data formatting | bytes 128
  37.3 0.6 %copy.9 = f32[2,768]{1,0:T(2,128)} copy(f32[2,768]{1,0:T(2,128)S(1)} %get-tuple-element.7) | data formatting | bytes 12288
